TPU v7x, 512 devices: a whole 4x8x8 slice. The times are simulated.
512 devices in a mesh: dp: 32 (over y, x), mp: 16 (over z, core).
Axes of the slice: x: 4, y: 8, z: 8, core: 2. Of those that a mesh axis runs over, the one named last changes fastest.
Arguments:
- grads: bfloat16 [32, 448, 17920], P('dp', None, 'mp'), may hold values from -6 to 6
- errors: bfloat16 [32, 448, 17920], P('dp', None, 'mp'), may hold values from -3 to 3
- q_start: float32 [17920, 128], P('mp'), may hold values from -0.046875 to 0.046875
Outputs:
- approx: bfloat16 [448, 17920], P(None, 'mp')
- q_next: float32 [17920, 128], P('mp')
- error_next: bfloat16 [32, 448, 17920], P('dp', None, 'mp')
All inputs are finite; a program needn't handle non-finite values.
Results may differ from a plain program's by a relative error of at most 0.0012.
Values sent between devices are 32-bit elements; how exact they have to be, the bound alone decides.
A program may use at most 64 MiB of HBM per device.

v0:
```python
import jax
import jax.numpy as jnp
from jax import lax
from jax.sharding import PartitionSpec as P


def local(grads, errors, q_start):
    highest = lax.Precision.HIGHEST
    replicas = lax.axis_size("dp")
    merged = grads[0].astype(jnp.float32) + errors[0].astype(jnp.float32)
    partial_value = jnp.dot(merged, q_start, precision=highest, preferred_element_type=jnp.float32)
    summed = lax.psum(partial_value, ("dp", "mp")) / replicas
    gram_matrix = jnp.dot(summed.T, summed, precision=highest, preferred_element_type=jnp.float32)
    factor_low = jnp.linalg.cholesky(gram_matrix)
    p_hat = lax.linalg.triangular_solve(
        factor_low, summed, left_side=False, lower=True, transpose_a=True
    )
    q_part = jnp.dot(merged.T, p_hat, precision=highest, preferred_element_type=jnp.float32)
    q_full = lax.psum(q_part, "dp") / replicas
    full_approx = jnp.dot(p_hat, q_full.T, precision=highest, preferred_element_type=jnp.float32)
    error_next = (merged - full_approx).astype(jnp.bfloat16)[None]
    return (full_approx.astype(jnp.bfloat16), q_full, error_next)


def solution(mesh):
    return jax.shard_map(
        local,
        mesh=mesh,
        in_specs=(P("dp", None, "mp"), P("dp", None, "mp"), P("mp", None)),
        out_specs=(P(None, "mp"), P("mp", None), P("dp", None, "mp")),
        check_vma=False,
    )
```

profile of v0, /device:TPU:64, one launch (start us, length us, event | category | flops | bytes accessed | tf_op | source)
XLA Modules:
  0.0 479.2 jit_solution(10909886290268158054)
XLA Ops:
  7.2 0.0 copy-start
  7.2 0.0 all-reduce.3.cloned.1.call-start
  7.2 1.0 copy-done
  8.2 0.0 copy-start.2
  8.2 4.3 fusion.2
  12.5 0.0 copy-start.1
  12.5 0.0 all-reduce.3.cloned.1.call-update
  12.5 0.0 all-reduce.5.cloned.1.call-start
  12.6 269.9 %all-reduce.3.cloned.1.call-done = f32[448,128]{1,0:T(8,128)} async-done(((f32[448,128]{1,0:T(8,128)}), f32[448,128]{1,0:T(8,128)}) %all-reduce.3.cloned.1.call-update) | async-done | bytes 229392 | tf_op jit(solution)/shard_map/psum | solution.py:12
  282.5 1.6 fusion.8
  284.1 0.1 copy.6
  284.2 11.7 %cholesky.16 = f32[128,128]{1,0:T(8,128)S(1)} custom-call(f32[128,128]{1,0:T(8,128)S(1)} %fusion.14), custom_call_target="Cholesky" | custom-call | tf_op jit(solution)/shard_map/jit(cholesky)/cholesky | solution.py:14
  296.0 0.6 compare_reduce_fusion
  296.6 0.7 fusion.12
  297.3 9.8 %custom-call.6 = f32[1,128,128]{1,2,0:T(8,128)S(1)} custom-call(f32[1,128,128]{2,1,0:T(8,128)S(1)} %fusion.12), custom_call_target="InvertDiagBlocksLowerTriangular" | custom-call | tf_op jit(solution)/shard_map/triangular_solve | solution.py:15
  307.1 1.3 fusion.6
  308.4 0.0 copy-done.2
  308.4 0.0 copy-done.1
  308.4 4.6 fusion
  313.1 0.0 all-reduce.5.cloned.1.call-update
  313.1 155.0 %all-reduce.5.cloned.1.call-done = f32[1120,128]{1,0:T(8,128)} async-done(((f32[1120,128]{1,0:T(8,128)}), f32[1120,128]{1,0:T(8,128)}) %all-reduce.5.cloned.1.call-update) | async-done | bytes 573456 | tf_op jit(solution)/shard_map/psum | solution.py:19
  468.1 1.1 broadcast_multiply_fusion
  469.2 0.0 copy-start.3
  469.2 3.2 fusion.5
  472.4 0.0 copy-done.3
  (2 shorter events, 0.0 us)
Async XLA Ops:
  7.2 1.1 copy-start
  7.2 275.3 %all-reduce.3.cloned.1.call-start = ((), (), s32[]{:S(2)}) async-start(), calls=%async_computation | async-start | bytes 458752 | tf_op jit(solution)/shard_map/psum | solution.py:12
  8.2 300.2 %copy-start.2 = (bf16[1,448,1120]{2,1,0:T(8,128)(2,1)S(1)}, bf16[1,448,1120]{2,1,0:T(8,128)(2,1)}, u32[]{:S(2)}) copy-start(bf16[1,448,1120]{2,1,0:T(8,128)(2,1)} %param.3) | copy-start | bytes 3010564
  12.5 295.9 %copy-start.1 = (bf16[1,448,1120]{2,1,0:T(8,128)(2,1)S(1)}, bf16[1,448,1120]{2,1,0:T(8,128)(2,1)}, u32[]{:S(2)}) copy-start(bf16[1,448,1120]{2,1,0:T(8,128)(2,1)} %param.4) | copy-start | bytes 3010564
  12.5 455.6 %all-reduce.5.cloned.1.call-start = ((), (), s32[]{:S(2)}) async-start(), calls=%async_computation.1 | async-start | bytes 1146880 | tf_op jit(solution)/shard_map/psum | solution.py:19
  469.2 3.2 copy-start.3
Sparse Core Ops, SparseCore 0:
  13.6 268.8 all-reduce.2
  313.2 154.8 all-reduce.4
where the time goes:
time: 480 us; the launch traced here: 479 us
  waiting for transfers between devices  425 us (89%)
  other arithmetic  24 us (5%)
  matrix products  15 us (3%)
  between operations  14.1 us (3%)
    psum x1, waiting for transfers between devices, local(): summed = lax.psum(partial_value, ('dp', 'mp')) / replicas  270 us
    psum x1, waiting for transfers between devices, local(): q_full = lax.psum(q_part, 'dp') / replicas  155 us
    another operation x3, other arithmetic, local(): factor_low = jnp.linalg.cholesky(gram_matrix)  12.4 us
    another operation x2, other arithmetic, local(): lax.linalg.triangular_solve(factor_low, summed, left_side=False, lower=Tr...  10.5 us
  transfers between devices with their start and end apart: 2, of which 2 were waited for; matrix products, arithmetic and copies ran while one was open for 0% of the time, Pallas kernels for 0%

commit v1 on v0

v1 whole, which is shorter than its diff:
```python
import functools

import jax
import jax.numpy as jnp
from jax import lax
from jax.experimental import pallas as pl
from jax.experimental.pallas import tpu as pltpu
from jax.sharding import PartitionSpec as P

MESH = pl.DeviceIdType.MESH
F32 = jnp.float32
BF16 = jnp.bfloat16

NX, NY, NZ, NC = 4, 8, 8, 2
OWNERS = 7
PIECE = 40
SPLIT = 32


def far_first(n):
    return sorted(range(1, n), key=lambda k: -min(k, n - k))


def near_first(n):
    return sorted(range(1, n), key=lambda k: min(k, n - k))


def dot(a, b, dims=((1,), (0,)), precision=None):
    return lax.dot_general(a, b, (dims, ((), ())), precision=precision, preferred_element_type=F32)


def halves(a):
    high = a.astype(BF16)
    return high, (a - high.astype(F32)).astype(BF16)


def panels(c, first, last):
    n = c.shape[0]

    def panel(index, c):
        rows = lax.broadcasted_iota(jnp.int32, (n, 1), 0)
        lanes = lax.broadcasted_iota(jnp.int32, (1, n), 1)
        inside = rows < n - 8 * index
        for j in range(8):
            inverse = 1.0 / c[j : j + 1, j : j + 1]
            row = c[j : j + 1, :] * inverse
            row = jnp.where(lanes == j, inverse, row)
            column = jnp.where((rows > j) & inside, c[:, j : j + 1], 0.0)
            below = (rows > j) & inside & (lanes == j)
            c = jnp.where(below, 0.0, c) - column * row
        c = pltpu.roll(c, n - 8, 1)
        return jnp.concatenate([c[8:], c[:8]], axis=0)

    return lax.fori_loop(first, last, panel, c)


def inverse_factor(c):
    n = c.shape[0]
    rows = lax.broadcasted_iota(jnp.int32, (n, n), 0)
    lanes = lax.broadcasted_iota(jnp.int32, (n, n), 1)
    pivots = jnp.sum(jnp.where(rows == lanes, c, 0.0), axis=1, keepdims=True)
    return jnp.where(lanes < rows, c, jnp.where(rows == lanes, 1.0, 0.0)) * lax.rsqrt(pivots)


def exchange(
    g_hbm, e_hbm, q_hbm, right_out, p_hat_out, inverse_out,
    g_v, e_v, q_v, gt_v, et_v, part_v, a_rx, by_rx, bz_rx, dz_rx, dy_rx, mean_v,
    qp_v, rx_rx, ry_v, ry_rx, right_v, c_v,
    load_sem, a_s, a_r, by_s, by_r, bz_s, bz_r, dz_s, dz_r, dy_s, dy_r, c_s, c_r,
    rx_s, rx_r, ry_s, ry_r, gy_s, gy_r, gx_s, gx_r,
):
    rows, width = g_v.shape
    chunk = rows // (NX * NC)
    cols = width // NX
    dp = lax.axis_index("dp")
    mp = lax.axis_index("mp")
    y, x, z, core = dp // NX, dp % NX, mp // NC, mp % NC

    def device(y, x, z, core):
        return (y * NX + x, z * NC + core)

    pending = []

    def send(src, dst, s, r, to):
        copy = pltpu.make_async_remote_copy(
            src_ref=src, dst_ref=dst, send_sem=s, recv_sem=r, device_id=to, device_id_type=MESH
        )
        copy.start()
        return copy

    loads = [
        pltpu.make_async_copy(src, dst, load_sem.at[i])
        for i, (src, dst) in enumerate(((q_hbm, q_v), (g_hbm, g_v), (e_hbm, e_v)))
    ]
    for load in loads:
        load.start()

    xc_offsets = [(dx, dc) for dx in far_first(NX) + [0] for dc in reversed(range(NC)) if (dx, dc) != (0, 0)]
    barrier = pltpu.get_barrier_semaphore()
    others = (
        [device((y + k) % NY, x, z, core) for k in far_first(NY)]
        + [device(y, x, (z + k) % NZ, core) for k in far_first(NZ)]
        + [device(y, (x + dx) % NX, z, (core + dc) % NC) for dx, dc in xc_offsets]
    )
    for other in others:
        pl.semaphore_signal(barrier, inc=1, device_id=other, device_id_type=MESH)

    loads[0].wait()
    q2 = jnp.concatenate(halves(q_v[...]), axis=1)
    loads[1].wait()
    loads[2].wait()
    both = dot(g_v[...], q2) + dot(e_v[...], q2)
    rank = q_v.shape[1]
    part_v[...] = both[:, :rank] + both[:, rank:]
    pl.semaphore_wait(barrier, len(others))

    mine = x * NC + core
    for k, (dx, dc) in enumerate(xc_offsets):
        x2, c2 = (x + dx) % NX, (core + dc) % NC
        src = part_v.at[pl.ds(pl.multiple_of((x2 * NC + c2) * chunk, 8), chunk)]
        pending.append(send(src, a_rx.at[k], a_s.at[k], a_r.at[k], device(y, x2, z, c2)))

    for start in range(0, width, 128):
        stop = min(start + 128, width)
        gt_v[start:stop, :] = g_v[:, start:stop].T
        et_v[start:stop, :] = e_v[:, start:stop].T

    total = part_v[pl.ds(pl.multiple_of(mine * chunk, 8), chunk), :]
    for k in range(len(xc_offsets)):
        pltpu.make_async_copy(a_rx.at[k], a_rx.at[k], a_r.at[k]).wait()
        total = total + a_rx[k]

    def spread_y(ref, s, r, k):
        y2 = (y + k) % NY
        return send(ref.at[y], ref.at[y], s.at[k - 1], r.at[k - 1], device(y2, x, z, core))

    def spread_z(ref, s, r, k):
        z2 = (z + k) % NZ
        return send(ref.at[z], ref.at[z], s.at[k - 1], r.at[k - 1], device(y, x, z2, core))

    def collect(ref, r, n):
        for k in range(1, n):
            pltpu.make_async_copy(ref.at[0], ref.at[0], r.at[k - 1]).wait()
        value = ref[0]
        for k in range(1, n):
            value = value + ref[k]
        return value

    by_rx[y] = total[:SPLIT]
    bz_rx[z] = total[SPLIT:]
    for ky, kz in zip(far_first(NY), far_first(NZ)):
        pending.append(spread_y(by_rx, by_s, by_r, ky))
        pending.append(spread_z(bz_rx, bz_s, bz_r, kz))
    dz_rx[z] = collect(by_rx, by_r, NY)
    for kz in far_first(NZ):
        pending.append(spread_z(dz_rx, dz_s, dz_r, kz))
    dy_rx[y] = collect(bz_rx, bz_r, NZ)
    for ky in far_first(NY):
        pending.append(spread_y(dy_rx, dy_s, dy_r, ky))
    first = collect(dz_rx, dz_r, NZ)
    second = collect(dy_rx, dy_r, NY)

    replicas = NX * NY
    mean_v[pl.ds(pl.multiple_of(mine * chunk, 8), SPLIT), :] = first / replicas
    mean_v[pl.ds(pl.multiple_of(mine * chunk + SPLIT, 8), chunk - SPLIT), :] = second / replicas
    own = mean_v.at[pl.ds(pl.multiple_of(mine * chunk, 8), chunk)]
    for k, (dx, dc) in enumerate(xc_offsets):
        x2, c2 = (x + dx) % NX, (core + dc) % NC
        pending.append(send(own, own, c_s.at[k], c_r.at[k], device(y, x2, z, c2)))
    for k in range(len(xc_offsets)):
        pltpu.make_async_copy(own, own, c_r.at[k]).wait()

    mean = mean_v[...]
    p2 = jnp.concatenate(halves(mean), axis=1)
    both = dot(gt_v[...], p2) + dot(et_v[...], p2)
    qp_v[...] = both[:, :rank] + both[:, rank:]

    def piece(x, y):
        return pl.ds(pl.multiple_of(x * cols + y * PIECE, 8), PIECE)

    def local_piece(y):
        return pl.ds(pl.multiple_of(y * PIECE, 8), PIECE)

    x_offsets = far_first(NX)
    for ky in far_first(NY) + [0]:
        y2 = (y + ky) % NY

        @pl.when(y2 < OWNERS)
        def _():
            for kx in x_offsets:
                x2 = (x + kx) % NX
                send(
                    qp_v.at[piece(x2, y2)], rx_rx.at[kx - 1, local_piece(y2)],
                    rx_s.at[kx - 1, ky], rx_r.at[kx - 1, ky], device(y, x2, z, core),
                )

    gram = dot(mean, mean, ((0,), (0,)), lax.Precision.HIGHEST)
    steps = gram.shape[0] // 8
    cut1, cut2 = steps // 4, steps * 5 // 8
    c_v[...] = panels(gram, 0, cut1)

    for ky in far_first(NY) + [0]:
        y2 = (y + ky) % NY

        @pl.when(y2 < OWNERS)
        def _():
            value = qp_v[piece(x, y2), :]
            for kx in x_offsets:
                got = rx_rx.at[kx - 1, local_piece(y2)]
                pltpu.make_async_copy(got, got, rx_r.at[kx - 1, ky]).wait()
                value = value + got[...]
            ry_v[local_piece(y2), :] = value
            if ky:
                send(ry_v.at[local_piece(y2)], ry_rx.at[ky - 1], ry_s.at[ky - 1], ry_r.at[ky - 1], device(y2, x, z, core))

    c_v[...] = panels(c_v[...], cut1, cut2)

    @pl.when(y < OWNERS)
    def _():
        value = ry_v[local_piece(y), :]
        for ky in near_first(NY):
            pltpu.make_async_copy(ry_rx.at[ky - 1], ry_rx.at[ky - 1], ry_r.at[ky - 1]).wait()
            value = value + ry_rx[ky - 1]
        right_v[piece(x, y), :] = value / replicas
        own = right_v.at[piece(x, y)]
        for ky in far_first(NY):
            send(own, own, gy_s.at[ky - 1], gy_r.at[ky - 1], device((y + ky) % NY, x, z, core))
        for kx in x_offsets:
            send(own, own, gx_s.at[kx - 1, 0], gx_r.at[kx - 1, 0], device(y, (x + kx) % NX, z, core))

    c_v[...] = panels(c_v[...], cut2, steps)

    for ky in near_first(NY):
        y2 = (y + NY - ky) % NY

        @pl.when(y2 < OWNERS)
        def _():
            got = right_v.at[piece(x, y2)]
            pltpu.make_async_copy(got, got, gy_r.at[ky - 1]).wait()
            for kx in x_offsets:
                send(got, got, gx_s.at[kx - 1, ky], gx_r.at[kx - 1, ky], device(y, (x + kx) % NX, z, core))

    inverse = inverse_factor(c_v[...])
    inverse_out[...] = inverse
    p_hat_out[...] = dot(mean, inverse, ((1,), (1,)), lax.Precision.HIGHEST)

    for copy in pending:
        copy.wait_send()
    for ky in range(NY):
        here = (y + ky) % NY
        there = (y + NY - ky) % NY

        @pl.when(here < OWNERS)
        def _():
            out = qp_v.at[piece(x, here)]
            for kx in x_offsets:
                pltpu.make_async_copy(out, out, rx_s.at[kx - 1, ky]).wait()
            if ky:
                pltpu.make_async_copy(out, out, ry_s.at[ky - 1]).wait()

        @pl.when(there < OWNERS)
        def _():
            out = right_v.at[piece(x, there)]
            for kx in x_offsets:
                pltpu.make_async_copy(out, out, gx_r.at[kx - 1, ky]).wait()
                pltpu.make_async_copy(out, out, gx_s.at[kx - 1, ky]).wait()

    @pl.when(y < OWNERS)
    def _():
        out = right_v.at[piece(x, y)]
        for ky in range(1, NY):
            pltpu.make_async_copy(out, out, gy_s.at[ky - 1]).wait()

    right_out[...] = right_v[...]


def finish(
    g_v, e_v, right_v, p_hat_v, inverse_v, approx_hbm, q_hbm, error_hbm,
    q_v, approx_v, error_v, q_sem, sems,
):
    rows = g_v.shape[0]
    block = 112 if rows % 112 == 0 else rows
    inverse_high, inverse_low = halves(inverse_v[...])
    high, low = halves(right_v[...])
    q_next = dot(
        jnp.concatenate([high, low, high], axis=1),
        jnp.concatenate([inverse_high, inverse_high, inverse_low], axis=1),
        ((1,), (1,)),
    )
    q_v[...] = q_next
    q_copy = pltpu.make_async_copy(q_v, q_hbm, q_sem)
    q_copy.start()
    q_high, q_low = halves(q_next)
    q3 = jnp.concatenate([q_high, q_high, q_low], axis=1)
    copies = [q_copy]
    for i in range(rows // block):
        part = pl.ds(i * block, block)
        p_high, p_low = halves(p_hat_v[part, :])
        full = dot(jnp.concatenate([p_high, p_low, p_high], axis=1), q3, ((1,), (1,)))
        approx_v[part, :] = full.astype(BF16)
        error_v[part, :] = (g_v[part, :].astype(F32) + e_v[part, :].astype(F32) - full).astype(BF16)
        for k, (src, dst) in enumerate(((approx_v, approx_hbm), (error_v, error_hbm))):
            copy = pltpu.make_async_copy(src.at[part], dst.at[part], sems.at[k, i])
            copy.start()
            copies.append(copy)
    for copy in copies:
        copy.wait()


def local(grads, errors, q_start):
    grads, errors = grads[0], errors[0]
    rows, width = grads.shape
    rank = q_start.shape[1]
    chunk = rows // (NX * NC)
    cols = width // NX
    nxc = NX * NC - 1
    anywhere = pl.BlockSpec(memory_space=pl.ANY)
    vmem = pl.BlockSpec(memory_space=pltpu.VMEM)
    dma = pltpu.SemaphoreType.DMA
    right, p_hat, inverse = pl.pallas_call(
        exchange,
        out_shape=(
            jax.ShapeDtypeStruct((width, rank), F32),
            jax.ShapeDtypeStruct((rows, rank), F32),
            jax.ShapeDtypeStruct((rank, rank), F32),
        ),
        in_specs=[anywhere] * 3,
        out_specs=(vmem,) * 3,
        scratch_shapes=[
            pltpu.VMEM((rows, width), BF16),
            pltpu.VMEM((rows, width), BF16),
            pltpu.VMEM((width, rank), F32),
            pltpu.VMEM((width, rows), BF16),
            pltpu.VMEM((width, rows), BF16),
            pltpu.VMEM((rows, rank), F32),
            pltpu.VMEM((nxc, chunk, rank), F32),
            pltpu.VMEM((NY, SPLIT, rank), F32),
            pltpu.VMEM((NZ, chunk - SPLIT, rank), F32),
            pltpu.VMEM((NZ, SPLIT, rank), F32),
            pltpu.VMEM((NY, chunk - SPLIT, rank), F32),
            pltpu.VMEM((rows, rank), F32),
            pltpu.VMEM((width, rank), F32),
            pltpu.VMEM((NX - 1, cols, rank), F32),
            pltpu.VMEM((cols, rank), F32),
            pltpu.VMEM((NY - 1, PIECE, rank), F32),
            pltpu.VMEM((width, rank), F32),
            pltpu.VMEM((rank, rank), F32),
            dma((3,)),
            dma((nxc,)), dma((nxc,)),
            dma((NY - 1,)), dma((NY - 1,)),
            dma((NZ - 1,)), dma((NZ - 1,)),
            dma((NZ - 1,)), dma((NZ - 1,)),
            dma((NY - 1,)), dma((NY - 1,)),
            dma((nxc,)), dma((nxc,)),
            dma((NX - 1, NY)), dma((NX - 1, NY)),
            dma((NY - 1,)), dma((NY - 1,)),
            dma((NY - 1,)), dma((NY - 1,)),
            dma((NX - 1, NY)), dma((NX - 1, NY)),
        ],
        compiler_params=pltpu.CompilerParams(
            collective_id=0, has_side_effects=True, vmem_limit_bytes=24 * 2**20
        ),
        name="exchange",
    )(grads, errors, q_start)

    block = 112 if rows % 112 == 0 else rows
    approx, q_next, error_next = pl.pallas_call(
        finish,
        out_shape=(
            jax.ShapeDtypeStruct((rows, width), BF16),
            jax.ShapeDtypeStruct((width, rank), F32),
            jax.ShapeDtypeStruct((rows, width), BF16),
        ),
        in_specs=[vmem] * 5,
        out_specs=(anywhere,) * 3,
        scratch_shapes=[
            pltpu.VMEM((width, rank), F32),
            pltpu.VMEM((rows, width), BF16),
            pltpu.VMEM((rows, width), BF16),
            dma,
            dma((2, rows // block)),
        ],
        compiler_params=pltpu.CompilerParams(vmem_limit_bytes=24 * 2**20),
        name="finish",
    )(grads, errors, right, p_hat, inverse)
    return approx, q_next, error_next[None]


def solution(mesh):
    return jax.shard_map(
        local,
        mesh=mesh,
        in_specs=(P("dp", None, "mp"), P("dp", None, "mp"), P("mp", None)),
        out_specs=(P(None, "mp"), P("mp", None), P("dp", None, "mp")),
        check_vma=False,
    )
```

time: 480 us -> 68.1 us (0.14)
  the two profiles are of different devices: /device:TPU:64 before, /device:TPU:1 now
where the time goes in v1:
time: 68.1 us; the launch traced here: 67.9 us
  Pallas kernels  63.8 us (94%)
  local copies, waits for them, and re-layouts  3.49 us (5%)
    pallas_call x1, Pallas kernels, local(): pl.pallas_call(exchange, out_shape=(jax.ShapeDtypeStruct((width, rank), F...  61.4 us
    unnamed x6, local copies, waits for them, and re-layouts  3.49 us
    pallas_call x1, Pallas kernels, local(): pl.pallas_call(finish, out_shape=(jax.ShapeDtypeStruct((rows, width), BF1...  2.41 us

profile of v1, /device:TPU:1, one launch (start us, length us, event | category | flops | bytes accessed | tf_op | source)
XLA Modules:
  0.0 67.9 jit_solution(12592701771974914962)
XLA Ops:
  0.6 0.0 copy-start
  0.6 1.2 %copy-done = bf16[1,448,1120]{2,1,0:T(8,128)(2,1)S(1)} copy-done((bf16[1,448,1120]{2,1,0:T(8,128)(2,1)S(1)}, bf16[1,448,1120]{2,1,0:T(8,128)(2,1)}, u32[]{:S(2)}) %copy-start) | copy-done | bytes 1003544
  1.9 0.0 copy-start.1
  1.9 1.2 %copy-done.1 = bf16[1,448,1120]{2,1,0:T(8,128)(2,1)S(1)} copy-done((bf16[1,448,1120]{2,1,0:T(8,128)(2,1)S(1)}, bf16[1,448,1120]{2,1,0:T(8,128)(2,1)}, u32[]{:S(2)}) %copy-start.1) | copy-done | bytes 1003544
  3.1 0.0 copy-start.2
  3.1 1.1 %copy-done.2 = f32[1120,128]{1,0:T(8,128)S(1)} copy-done((f32[1120,128]{1,0:T(8,128)S(1)}, f32[1120,128]{1,0:T(8,128)}, u32[]{:S(2)}) %copy-start.2) | copy-done | bytes 573464
  4.1 61.4 %exchange.1 = (f32[1120,128]{1,0:T(8,128)S(1)}, f32[448,128]{1,0:T(8,128)S(1)}, f32[128,128]{1,0:T(8,128)S(1)}) custom-call(bf16[448,1120]{1,0:T(8,128)(2,1)S(1)} %bitcast.3, bf16[448,1120]{1,0:T(8,128)(2,1)S(1)} %bitcast.5, f32[1120,128]{1,0:T(8,128)S(1)} %copy-done.2), custom_call_target="tpu_custom_call" | custom-call | tf_op jit(solution)/shard_map/exchange/pallas_call | solution.py:320
  65.5 2.4 %finish.1 = (bf16[448,1120]{1,0:T(8,128)(2,1)}, f32[1120,128]{1,0:T(8,128)}, bf16[448,1120]{1,0:T(8,128)(2,1)}) custom-call(bf16[448,1120]{1,0:T(8,128)(2,1)S(1)} %bitcast.4, bf16[448,1120]{1,0:T(8,128)(2,1)S(1)} %bitcast.6, f32[1120,128]{1,0:T(8,128)S(1)} %get-tuple-element.9.right_v, f32[448,128]{1,0:T(8,128)S(1)} %get-tuple-element.10.p_hat_v, ...), custom_call_target="tpu_custom_call" | custom-call | tf_op jit(solution)/shard_map/finish/pallas_call | solution.py:367
Async XLA Ops:
  0.6 1.2 %copy-start = (bf16[1,448,1120]{2,1,0:T(8,128)(2,1)S(1)}, bf16[1,448,1120]{2,1,0:T(8,128)(2,1)}, u32[]{:S(2)}) copy-start(bf16[1,448,1120]{2,1,0:T(8,128)(2,1)} %param.3) | copy-start | bytes 3010564
  1.9 1.2 %copy-start.1 = (bf16[1,448,1120]{2,1,0:T(8,128)(2,1)S(1)}, bf16[1,448,1120]{2,1,0:T(8,128)(2,1)}, u32[]{:S(2)}) copy-start(bf16[1,448,1120]{2,1,0:T(8,128)(2,1)} %param.4) | copy-start | bytes 3010564
  3.1 1.1 %copy-start.2 = (f32[1120,128]{1,0:T(8,128)S(1)}, f32[1120,128]{1,0:T(8,128)}, u32[]{:S(2)}) copy-start(f32[1120,128]{1,0:T(8,128)} %q_hbm.1) | copy-start | bytes 1720324

commit v2 on v0

v2 whole, which is shorter than its diff:
```python
import functools

import jax
import jax.numpy as jnp
from jax import lax
from jax.experimental import pallas as pl
from jax.experimental.pallas import tpu as pltpu
from jax.sharding import PartitionSpec as P

MESH = pl.DeviceIdType.MESH
F32 = jnp.float32
BF16 = jnp.bfloat16

NX, NY, NZ, NC = 4, 8, 8, 2
OWNERS = 7
PIECE = 40
SPLIT = 32
BLOCK = 112
TALL = 224
LIMIT = 53 * 2**20


def loop(n, body):
    def step(i, carry):
        body(i)
        return carry

    lax.fori_loop(0, n, step, 0)


def far_first(i, n):
    return n // 2 + (i + 1) // 2 * (1 - 2 * (i % 2))


def dot(a, b, dims=((1,), (0,)), precision=None):
    return lax.dot_general(a, b, (dims, ((), ())), precision=precision, preferred_element_type=F32)


def halves(a):
    high = a.astype(BF16)
    return high, (a - high.astype(F32)).astype(BF16)


def span(start, size, unit=8):
    return pl.ds(pl.multiple_of(start, unit), size)


def panel(index, c):
    n = c.shape[0]
    rows = lax.broadcasted_iota(jnp.int32, (n, 1), 0)
    lanes = lax.broadcasted_iota(jnp.int32, (1, n), 1)
    inside = rows < n - 8 * index
    for j in range(8):
        inverse = 1.0 / c[j : j + 1, j : j + 1]
        row = c[j : j + 1, :] * inverse
        row = jnp.where(lanes == j, inverse, row)
        below = (rows > j) & inside
        column = jnp.where(below, c[:, j : j + 1], 0.0)
        c = jnp.where(below & (lanes == j), 0.0, c) - column * row
    c = pltpu.roll(c, n - 8, 1)
    return jnp.concatenate([c[8:], c[:8]], axis=0)


def inverse_factor(c):
    n = c.shape[0]
    rows = lax.broadcasted_iota(jnp.int32, (n, n), 0)
    lanes = lax.broadcasted_iota(jnp.int32, (n, n), 1)
    pivots = jnp.sum(jnp.where(rows == lanes, c, 0.0), axis=1, keepdims=True)
    return jnp.where(lanes < rows, c, jnp.where(rows == lanes, 1.0, 0.0)) * lax.rsqrt(pivots)


def exchange(
    g_hbm, e_hbm, q_hbm, right_out, p_hat_out, inverse_out,
    m_v, q_v, t_v, part_v, a_rx, by_rx, bz_rx, dz_rx, dy_rx, mean_v, p2_v,
    qp_v, rx_rx, ry_v, ry_rx, right_v, c_v,
    load_sem, a_s, a_r, by_s, by_r, bz_s, bz_r, dz_s, dz_r, dy_s, dy_r, c_s, c_r,
    rx_s, rx_r, ry_s, ry_r, gy_s, gy_r, gx_s, gx_r,
):
    _, rows, width = m_v.shape
    rank = q_v.shape[1]
    chunk = rows // (NX * NC)
    cols = width // NX
    replicas = NX * NY
    dp = lax.axis_index("dp")
    mp = lax.axis_index("mp")
    y, x, z, core = dp // NX, dp % NX, mp // NC, mp % NC

    def device(y, x, z, core):
        return (y * NX + x, z * NC + core)

    def send(src, dst, s, r, to):
        pltpu.make_async_remote_copy(
            src_ref=src, dst_ref=dst, send_sem=s, recv_sem=r, device_id=to, device_id_type=MESH
        ).start()

    def wait(ref, sem):
        pltpu.make_async_copy(ref, ref, sem).wait()

    def along_y(i):
        k = far_first(i, NY)
        return k, device((y + k) % NY, x, z, core)

    def along_z(i):
        k = far_first(i, NZ)
        return k, device(y, x, (z + k) % NZ, core)

    def across(i):
        x2 = (x + far_first(i // NC, NX)) % NX
        c2 = (core + NC - 1 - i % NC) % NC
        return x2 * NC + c2, device(y, x2, z, c2)

    loads = [
        pltpu.make_async_copy(src, dst, load_sem.at[i])
        for i, (src, dst) in enumerate(((q_hbm, q_v), (g_hbm, m_v.at[0]), (e_hbm, m_v.at[1])))
    ]
    for load in loads:
        load.start()

    barrier = pltpu.get_barrier_semaphore()

    def greet(to):
        pl.semaphore_signal(barrier, inc=1, device_id=to, device_id_type=MESH)

    loop(NY - 1, lambda i: greet(along_y(i)[1]))
    loop(NZ - 1, lambda i: greet(along_z(i)[1]))
    loop(NX * NC - 1, lambda i: greet(across(i)[1]))

    for load in loads:
        load.wait()
    q2 = jnp.concatenate(halves(q_v[...]), axis=1)

    def left_rows(i):
        block = span(i * BLOCK, BLOCK, 16)
        both = dot(m_v[0, block, :], q2) + dot(m_v[1, block, :], q2)
        part_v[block, :] = both[:, :rank] + both[:, rank:]

    loop(rows // BLOCK, left_rows)
    pl.semaphore_wait(barrier, NY + NZ + NX * NC - 3)

    mine = x * NC + core

    def scatter(i):
        other, to = across(i)
        send(part_v.at[span(other * chunk, chunk)], a_rx.at[i], a_s.at[i], a_r.at[i], to)

    loop(NX * NC - 1, scatter)

    full = width // 128

    def turn(i):
        at = span(i % full * 128, 128, 128)
        t_v[i // full, at, :] = m_v[i // full, :, at].T

    loop(2 * full, turn)
    if width % 128:

        def turn_rest(i):
            t_v[i, full * 128 :, :] = m_v[i, :, full * 128 :].T

        loop(2, turn_rest)

    def add_chunk(i, total):
        wait(a_rx.at[i], a_r.at[i])
        return total + a_rx[i]

    total = lax.fori_loop(0, NX * NC - 1, add_chunk, part_v[span(mine * chunk, chunk), :])

    def spread_y(ref, s, r):
        def step(i):
            k, to = along_y(i)
            send(ref.at[y], ref.at[y], s.at[k - 1], r.at[k - 1], to)

        return step

    def spread_z(ref, s, r):
        def step(i):
            k, to = along_z(i)
            send(ref.at[z], ref.at[z], s.at[k - 1], r.at[k - 1], to)

        return step

    def collect(ref, r):
        n = ref.shape[0]
        loop(n - 1, lambda i: wait(ref.at[0], r.at[i]))
        value = ref[0]
        for k in range(1, n):
            value = value + ref[k]
        return value

    by_rx[y] = total[:SPLIT]
    bz_rx[z] = total[SPLIT:]
    loop(NY - 1, spread_y(by_rx, by_s, by_r))
    loop(NZ - 1, spread_z(bz_rx, bz_s, bz_r))
    dz_rx[z] = collect(by_rx, by_r)
    loop(NZ - 1, spread_z(dz_rx, dz_s, dz_r))
    dy_rx[y] = collect(bz_rx, bz_r)
    loop(NY - 1, spread_y(dy_rx, dy_s, dy_r))
    mean_v[span(mine * chunk, SPLIT), :] = collect(dz_rx, dz_r) / replicas
    mean_v[span(mine * chunk + SPLIT, chunk - SPLIT), :] = collect(dy_rx, dy_r) / replicas

    own = mean_v.at[span(mine * chunk, chunk)]
    loop(NX * NC - 1, lambda i: send(own, own, c_s.at[i], c_r.at[i], across(i)[1]))
    loop(NX * NC - 1, lambda i: wait(own, c_r.at[i]))

    p2_v[...] = jnp.concatenate(halves(mean_v[...]), axis=1)

    def right_rows(i):
        block = span(i * TALL, TALL, 16)
        both = dot(t_v[0, block, :], p2_v[...]) + dot(t_v[1, block, :], p2_v[...])
        qp_v[block, :] = both[:, :rank] + both[:, rank:]

    loop(width // TALL, right_rows)

    def piece(x, y):
        return span(x * cols + y * PIECE, PIECE)

    def local_piece(y):
        return span(y * PIECE, PIECE)

    def along_x(i):
        k = far_first(i, NX)
        return k - 1, (x + k) % NX, device(y, (x + k) % NX, z, core)

    def scatter_x(i):
        ky = far_first(i, NY)
        y2 = (y + ky) % NY

        @pl.when(y2 < OWNERS)
        def _():
            def step(j):
                kx, x2, to = along_x(j)
                send(qp_v.at[piece(x2, y2)], rx_rx.at[kx, local_piece(y2)], rx_s.at[kx, ky], rx_r.at[kx, ky], to)

            loop(NX - 1, step)

    loop(NY, scatter_x)

    mean = mean_v[...]
    c_v[...] = dot(mean, mean, ((0,), (0,)), lax.Precision.HIGHEST)

    def scatter_y(i):
        ky = far_first(i, NY)
        y2 = (y + ky) % NY

        @pl.when(y2 < OWNERS)
        def _():
            value = qp_v[piece(x, y2), :]
            for kx in range(NX - 1):
                wait(rx_rx.at[kx, local_piece(y2)], rx_r.at[kx, ky])
                value = value + rx_rx[kx, local_piece(y2), :]
            ry_v[local_piece(y2), :] = value

            @pl.when(ky > 0)
            def _():
                send(ry_v.at[local_piece(y2)], ry_rx.at[ky - 1], ry_s.at[ky - 1], ry_r.at[ky - 1], along_y(i)[1])

    def own_piece():
        def add(i, value):
            wait(ry_rx.at[i], ry_r.at[i])
            return value + ry_rx[i]

        right_v[piece(x, y), :] = lax.fori_loop(0, NY - 1, add, ry_v[local_piece(y), :]) / replicas
        out = right_v.at[piece(x, y)]

        def to_y(i):
            k, to = along_y(i)
            send(out, out, gy_s.at[k - 1], gy_r.at[k - 1], to)

        def to_x(j):
            kx, _, to = along_x(j)
            send(out, out, gx_s.at[kx, 0], gx_r.at[kx, 0], to)

        loop(NY - 1, to_y)
        loop(NX - 1, to_x)

    def gather(i):
        ky = far_first(NY - 2 - i, NY)
        y2 = (y + NY - ky) % NY

        @pl.when(y2 < OWNERS)
        def _():
            got = right_v.at[piece(x, y2)]
            wait(got, gy_r.at[ky - 1])

            def step(j):
                kx, _, to = along_x(j)
                send(got, got, gx_s.at[kx, ky], gx_r.at[kx, ky], to)

            loop(NX - 1, step)

    steps = rank // 8
    cut1, cut2 = steps // 4, steps * 5 // 8

    def stage(s):
        first = jnp.where(s == 0, 0, jnp.where(s == 1, cut1, cut2))
        last = jnp.where(s == 0, cut1, jnp.where(s == 1, cut2, steps))
        c_v[...] = lax.fori_loop(first, last, panel, c_v[...])

        @pl.when(s == 0)
        def _():
            loop(NY, scatter_y)

        @pl.when((s == 1) & (y < OWNERS))
        def _():
            own_piece()

        @pl.when(s == 2)
        def _():
            loop(NY - 1, gather)

    loop(3, stage)

    inverse = inverse_factor(c_v[...])
    inverse_out[...] = inverse
    p_hat_out[...] = dot(mean_v[...], inverse, ((1,), (1,)), lax.Precision.HIGHEST)

    def done_across(i):
        wait(own, a_s.at[i])
        wait(own, c_s.at[i])

    def done_y(i):
        wait(by_rx.at[0], by_s.at[i])
        wait(dy_rx.at[0], dy_s.at[i])

    def done_z(i):
        wait(bz_rx.at[0], bz_s.at[i])
        wait(dz_rx.at[0], dz_s.at[i])

    loop(NX * NC - 1, done_across)
    loop(NY - 1, done_y)
    loop(NZ - 1, done_z)
    one = right_v.at[span(0, PIECE)]

    def done_pieces(ky):
        @pl.when((y + ky) % NY < OWNERS)
        def _():
            loop(NX - 1, lambda kx: wait(one, rx_s.at[kx, ky]))

            @pl.when(ky > 0)
            def _():
                wait(one, ry_s.at[ky - 1])

        @pl.when((y + NY - ky) % NY < OWNERS)
        def _():
            def step(kx):
                wait(one, gx_r.at[kx, ky])
                wait(one, gx_s.at[kx, ky])

            loop(NX - 1, step)

        @pl.when((ky > 0) & (y < OWNERS))
        def _():
            wait(one, gy_s.at[ky - 1])

    loop(NY, done_pieces)
    right_out[...] = right_v[...]


def finish(
    g_hbm, e_hbm, right_v, p_hat_v, inverse_v, approx_hbm, q_hbm, error_hbm,
    m_v, q_v, q3_v, approx_v, error_v, load_sem, q_sem, sems,
):
    _, rows, width = m_v.shape
    loads = [pltpu.make_async_copy(src, m_v.at[i], load_sem.at[i]) for i, src in enumerate((g_hbm, e_hbm))]
    for load in loads:
        load.start()
    inverse_high, inverse_low = halves(inverse_v[...])
    inverse3 = jnp.concatenate([inverse_high, inverse_high, inverse_low], axis=1)

    def right_rows(i):
        block = span(i * TALL, TALL, 16)
        high, low = halves(right_v[block, :])
        q_next = dot(jnp.concatenate([high, low, high], axis=1), inverse3, ((1,), (1,)))
        q_v[block, :] = q_next
        high, low = halves(q_next)
        q3_v[block, :] = jnp.concatenate([high, high, low], axis=1)

    loop(width // TALL, right_rows)
    q_copy = pltpu.make_async_copy(q_v, q_hbm, q_sem)
    q_copy.start()
    for load in loads:
        load.wait()

    def left_rows(i):
        block = span(i * BLOCK, BLOCK, 16)
        high, low = halves(p_hat_v[block, :])
        full = dot(jnp.concatenate([high, low, high], axis=1), q3_v[...], ((1,), (1,)))
        approx_v[block, :] = full.astype(BF16)
        error_v[block, :] = (m_v[0, block, :].astype(F32) + m_v[1, block, :].astype(F32) - full).astype(BF16)
        pltpu.make_async_copy(approx_v.at[block], approx_hbm.at[block], sems.at[0, i]).start()
        pltpu.make_async_copy(error_v.at[block], error_hbm.at[block], sems.at[1, i]).start()

    def done(i):
        block = span(i * BLOCK, BLOCK, 16)
        pltpu.make_async_copy(approx_v.at[block], approx_hbm.at[block], sems.at[0, i]).wait()
        pltpu.make_async_copy(error_v.at[block], error_hbm.at[block], sems.at[1, i]).wait()

    loop(rows // BLOCK, left_rows)
    loop(rows // BLOCK, done)
    q_copy.wait()


def local(grads, errors, q_start):
    grads, errors = grads[0], errors[0]
    rows, width = grads.shape
    rank = q_start.shape[1]
    chunk = rows // (NX * NC)
    cols = width // NX
    nxc = NX * NC - 1
    anywhere = pl.BlockSpec(memory_space=pl.ANY)
    vmem = pl.BlockSpec(memory_space=pltpu.VMEM)
    dma = pltpu.SemaphoreType.DMA
    right, p_hat, inverse = pl.pallas_call(
        exchange,
        out_shape=(
            jax.ShapeDtypeStruct((width, rank), F32),
            jax.ShapeDtypeStruct((rows, rank), F32),
            jax.ShapeDtypeStruct((rank, rank), F32),
        ),
        in_specs=[anywhere] * 3,
        out_specs=(vmem,) * 3,
        scratch_shapes=[
            pltpu.VMEM((2, rows, width), BF16),
            pltpu.VMEM((width, rank), F32),
            pltpu.VMEM((2, width, rows), BF16),
            pltpu.VMEM((rows, rank), F32),
            pltpu.VMEM((nxc, chunk, rank), F32),
            pltpu.VMEM((NY, SPLIT, rank), F32),
            pltpu.VMEM((NZ, chunk - SPLIT, rank), F32),
            pltpu.VMEM((NZ, SPLIT, rank), F32),
            pltpu.VMEM((NY, chunk - SPLIT, rank), F32),
            pltpu.VMEM((rows, rank), F32),
            pltpu.VMEM((rows, 2 * rank), BF16),
            pltpu.VMEM((width, rank), F32),
            pltpu.VMEM((NX - 1, cols, rank), F32),
            pltpu.VMEM((cols, rank), F32),
            pltpu.VMEM((NY - 1, PIECE, rank), F32),
            pltpu.VMEM((width, rank), F32),
            pltpu.VMEM((rank, rank), F32),
            dma((3,)),
            dma((nxc,)), dma((nxc,)),
            dma((NY - 1,)), dma((NY - 1,)),
            dma((NZ - 1,)), dma((NZ - 1,)),
            dma((NZ - 1,)), dma((NZ - 1,)),
            dma((NY - 1,)), dma((NY - 1,)),
            dma((nxc,)), dma((nxc,)),
            dma((NX - 1, NY)), dma((NX - 1, NY)),
            dma((NY - 1,)), dma((NY - 1,)),
            dma((NY - 1,)), dma((NY - 1,)),
            dma((NX - 1, NY)), dma((NX - 1, NY)),
        ],
        compiler_params=pltpu.CompilerParams(collective_id=0, has_side_effects=True, vmem_limit_bytes=LIMIT),
        name="exchange",
    )(grads, errors, q_start)

    approx, q_next, error_next = pl.pallas_call(
        finish,
        out_shape=(
            jax.ShapeDtypeStruct((rows, width), BF16),
            jax.ShapeDtypeStruct((width, rank), F32),
            jax.ShapeDtypeStruct((rows, width), BF16),
        ),
        in_specs=[anywhere] * 2 + [vmem] * 3,
        out_specs=(anywhere,) * 3,
        scratch_shapes=[
            pltpu.VMEM((2, rows, width), BF16),
            pltpu.VMEM((width, rank), F32),
            pltpu.VMEM((width, 3 * rank), BF16),
            pltpu.VMEM((rows, width), BF16),
            pltpu.VMEM((rows, width), BF16),
            dma((2,)),
            dma,
            dma((2, rows // BLOCK)),
        ],
        compiler_params=pltpu.CompilerParams(vmem_limit_bytes=LIMIT),
        name="finish",
    )(grads, errors, right, p_hat, inverse)
    return approx, q_next, error_next[None]


def solution(mesh):
    return jax.shard_map(
        local,
        mesh=mesh,
        in_specs=(P("dp", None, "mp"), P("dp", None, "mp"), P("mp", None)),
        out_specs=(P(None, "mp"), P("mp", None), P("dp", None, "mp")),
        check_vma=False,
    )
```

time: 480 us -> 65.9 us (0.14)
  the two profiles are of different devices: /device:TPU:64 before, /device:TPU:2 now
where the time goes in v2:
time: 65.9 us; the launch traced here: 65.7 us
  Pallas kernels  65.1 us (99%)
    pallas_call x1, Pallas kernels, local(): pl.pallas_call(exchange, out_shape=(jax.ShapeDtypeStruct((width, rank), F...  61 us
    pallas_call x1, Pallas kernels, local(): pl.pallas_call(finish, out_shape=(jax.ShapeDtypeStruct((rows, width), BF1...  4.04 us

profile of v2, /device:TPU:2, one launch (start us, length us, event | category | flops | bytes accessed | tf_op | source)
XLA Modules:
  0.0 65.7 jit_solution(13783828888980193229)
XLA Ops:
  0.6 61.0 %exchange.1 = (f32[1120,128]{1,0:T(8,128)S(1)}, f32[448,128]{1,0:T(8,128)S(1)}, f32[128,128]{1,0:T(8,128)S(1)}) custom-call(bf16[448,1120]{1,0:T(8,128)(2,1)} %bitcast.3, bf16[448,1120]{1,0:T(8,128)(2,1)} %bitcast.5, f32[1120,128]{1,0:T(8,128)} %q_hbm.1), custom_call_target="tpu_custom_call" | custom-call | tf_op jit(solution)/shard_map/exchange/pallas_call | solution.py:413
  61.7 4.0 %finish.1 = (bf16[448,1120]{1,0:T(8,128)(2,1)}, f32[1120,128]{1,0:T(8,128)}, bf16[448,1120]{1,0:T(8,128)(2,1)}) custom-call(bf16[448,1120]{1,0:T(8,128)(2,1)} %bitcast.4, bf16[448,1120]{1,0:T(8,128)(2,1)} %bitcast.6, f32[1120,128]{1,0:T(8,128)S(1)} %get-tuple-element.9.right_v, f32[448,128]{1,0:T(8,128)S(1)} %get-tuple-element.10.p_hat_v, ...), custom_call_target="tpu_custom_call" | custom-call | tf_op jit(solution)/shard_map/finish/pallas_call | solution.py:456

commit v3 on v2

v3 whole, which is shorter than its diff:
```python
import functools

import jax
import jax.numpy as jnp
from jax import lax
from jax.experimental import pallas as pl
from jax.experimental.pallas import tpu as pltpu
from jax.sharding import PartitionSpec as P

MESH = pl.DeviceIdType.MESH
F32 = jnp.float32
BF16 = jnp.bfloat16

NX, NY, NZ, NC = 4, 8, 8, 2
OWNERS = 7
PIECE = 40
SPLIT = 32
BLOCK = 112
TALL = 224
FIRST = 3
LIMIT = 53 * 2**20


def loop(n, body):
    def step(i, carry):
        body(i)
        return carry

    lax.fori_loop(0, n, step, 0)


def far_first(i, n):
    return n // 2 + (i + 1) // 2 * (1 - 2 * (i % 2))


def dot(a, b, dims=((1,), (0,)), precision=None):
    return lax.dot_general(a, b, (dims, ((), ())), precision=precision, preferred_element_type=F32)


def halves(a):
    high = a.astype(BF16)
    return high, (a - high.astype(F32)).astype(BF16)


def span(start, size, unit=8):
    return pl.ds(pl.multiple_of(start, unit), size)


def panel(index, c):
    n = c.shape[0]
    lanes = lax.broadcasted_iota(jnp.int32, (1, n), 1)
    rows = lax.broadcasted_iota(jnp.int32, (n, 1), 0)
    active = rows < n - 8 * index
    live = jnp.where(active, c, 0.0)
    top = c[:8, :]

    def copies(row):
        return jnp.broadcast_to(row, (8, n))

    heads = [jnp.broadcast_to(top[:, k : k + 1], (8, n)) for k in range(8)]
    columns = [jnp.broadcast_to(live[8:, k : k + 1], (n - 8, n)) for k in range(8)]
    left = {(i, k): copies(heads[k][i : i + 1, :]) for k in range(8) for i in range(k, 8)}
    lower, scale = {}, []
    for j in range(8):
        scale.append(lax.rsqrt(left[j, j]))
        for i in range(j + 1, 8):
            lower[i, j] = left[i, j] * scale[j]
        for k in range(j + 1, 8):
            for i in range(k, 8):
                left[i, k] = left[i, k] - lower[i, j] * lower[k, j]
    done = []
    for j in range(8):
        value = copies(jnp.where(lanes < 8, jnp.where(lanes == j, 1.0, 0.0), top[j : j + 1, :]))
        for k in range(j):
            value = value - lower[j, k] * done[k]
        done.append(value * scale[j])
    solved = [None] * 8
    for k in reversed(range(8)):
        value = done[k]
        for j in range(k + 1, 8):
            value = value - lower[j, k] * solved[j]
        solved[k] = value * scale[k]
    rest = jnp.where(active[8:] & (lanes < 8), 0.0, c[8:])
    for k in range(8):
        rest = rest - columns[k] * solved[k][:1]
    top = jnp.concatenate([row[:1] for row in done], axis=0)
    return jnp.concatenate([pltpu.roll(rest, n - 8, 1), pltpu.roll(top, n - 8, 1)], axis=0)


def inverse_factor(c):
    n = c.shape[0]
    rows = lax.broadcasted_iota(jnp.int32, (n, n), 0)
    lanes = lax.broadcasted_iota(jnp.int32, (n, n), 1)
    return jnp.where(lanes <= rows, c, 0.0)


def times_transposed(a, b):
    a_high, a_low = halves(a)
    b_high, b_low = halves(b)
    return dot(
        jnp.concatenate([a_high, a_low, a_high], axis=1), jnp.concatenate([b_high, b_high, b_low], axis=1), ((1,), (1,))
    )


def exchange(
    g_hbm, e_hbm, q_hbm, right_out, p_hat_out,
    m_v, q_v, t_v, part_v, a_rx, by_rx, bz_rx, dz_rx, dy_rx, mean_v, p2_v,
    qp_v, rx_rx, ry_v, ry_rx, right_v, c_v,
    load_sem, a_s, a_r, by_s, by_r, bz_s, bz_r, dz_s, dz_r, dy_s, dy_r, c_s, c_r,
    rx_s, rx_r, ry_s, ry_r, gy_s, gy_r, gx_s, gx_r,
):
    _, rows, width = m_v.shape
    rank = q_v.shape[1]
    chunk = rows // (NX * NC)
    cols = width // NX
    replicas = NX * NY
    nxc = NX * NC
    dp = lax.axis_index("dp")
    mp = lax.axis_index("mp")
    y, x, z, core = dp // NX, dp % NX, mp // NC, mp % NC

    def device(y, x, z, core):
        return (y * NX + x, z * NC + core)

    def send(src, dst, s, r, to):
        pltpu.make_async_remote_copy(
            src_ref=src, dst_ref=dst, send_sem=s, recv_sem=r, device_id=to, device_id_type=MESH
        ).start()

    def wait(ref, sem):
        pltpu.make_async_copy(ref, ref, sem).wait()

    def along_y(i):
        k = far_first(i, NY)
        return k, device((y + k) % NY, x, z, core)

    def along_z(i):
        k = far_first(i, NZ)
        return k, device(y, x, (z + k) % NZ, core)

    def across(i):
        x2 = (x + far_first(i // NC, NX)) % NX
        c2 = (core + NC - 1 - i % NC) % NC
        return x2 * NC + c2, device(y, x2, z, c2)

    loads = [
        pltpu.make_async_copy(src, dst, load_sem.at[i])
        for i, (src, dst) in enumerate(((q_hbm, q_v), (g_hbm, m_v.at[0]), (e_hbm, m_v.at[1])))
    ]
    for load in loads:
        load.start()

    barrier = pltpu.get_barrier_semaphore()

    def greet(to):
        pl.semaphore_signal(barrier, inc=1, device_id=to, device_id_type=MESH)

    loop(max(NY, NZ) - 1, lambda i: (greet(along_y(i)[1]), greet(along_z(i)[1])))
    loop(nxc - 1, lambda i: greet(across(i)[1]))

    for load in loads:
        load.wait()
    q2 = jnp.concatenate(halves(q_v[...]), axis=1)

    def left_rows(i):
        block = span(i * BLOCK, BLOCK, 16)
        both = dot(m_v[0, block, :], q2) + dot(m_v[1, block, :], q2)
        part_v[block, :] = both[:, :rank] + both[:, rank:]

    loop(rows // BLOCK, left_rows)

    pl.semaphore_wait(barrier, NY + NZ + nxc - 3)

    mine = x * NC + core

    def scatter(i):
        other, to = across(i)
        send(part_v.at[span(other * chunk, chunk)], a_rx.at[i], a_s, a_r.at[i], to)

    loop(nxc - 1, scatter)

    full = width // 128

    def turn(i):
        at = span(i % full * 128, 128, 128)
        t_v[i // full, at, :] = m_v[i // full, :, at].T

    loop(2 * full, turn)
    if width % 128:

        def turn_rest(i):
            t_v[i, full * 128 :, :] = m_v[i, :, full * 128 :].T

        loop(2, turn_rest)

    def add_chunk(i, total):
        wait(a_rx.at[i], a_r.at[i])
        return total + a_rx[i]

    total = lax.fori_loop(0, nxc - 1, add_chunk, part_v[span(mine * chunk, chunk), :])

    def spread_y(ref, s, r, i):
        send(ref.at[y], ref.at[y], s, r, along_y(i)[1])

    def spread_z(ref, s, r, i):
        send(ref.at[z], ref.at[z], s, r, along_z(i)[1])

    def collect(ref, r):
        n = ref.shape[0]
        wait(ref.at[: n - 1], r)
        value = ref[0]
        for k in range(1, n):
            value = value + ref[k]
        return value

    by_rx[y] = total[:SPLIT]
    bz_rx[z] = total[SPLIT:]

    def spread(i):
        spread_y(by_rx, by_s, by_r, i)
        spread_z(bz_rx, bz_s, bz_r, i)

    loop(max(NY, NZ) - 1, spread)
    dz_rx[z] = collect(by_rx, by_r)
    loop(NZ - 1, functools.partial(spread_z, dz_rx, dz_s, dz_r))
    dy_rx[y] = collect(bz_rx, bz_r)
    loop(NY - 1, functools.partial(spread_y, dy_rx, dy_s, dy_r))
    mean_v[span(mine * chunk, SPLIT), :] = collect(dz_rx, dz_r) / replicas
    mean_v[span(mine * chunk + SPLIT, chunk - SPLIT), :] = collect(dy_rx, dy_r) / replicas

    own = mean_v.at[span(mine * chunk, chunk)]
    loop(nxc - 1, lambda i: send(own, own, c_s, c_r, across(i)[1]))

    wait(part_v.at[pl.ds(0, (nxc - 1) * chunk)], a_s)
    wait(by_rx.at[: NY - 1], by_s)
    wait(bz_rx.at[: NZ - 1], bz_s)
    wait(dz_rx.at[: NZ - 1], dz_s)
    wait(dy_rx.at[: NY - 1], dy_s)
    wait(mean_v.at[pl.ds(0, (nxc - 1) * chunk)], c_r)
    wait(mean_v.at[pl.ds(0, (nxc - 1) * chunk)], c_s)
    p2_v[...] = jnp.concatenate(halves(mean_v[...]), axis=1)

    def right_rows(i):
        block = span(i * TALL, TALL, 16)
        both = dot(t_v[0, block, :], p2_v[...]) + dot(t_v[1, block, :], p2_v[...])
        qp_v[block, :] = both[:, :rank] + both[:, rank:]

    loop(width // TALL, right_rows)

    def piece(x, y):
        return span(x * cols + y * PIECE, PIECE)

    def local_piece(y):
        return span(y * PIECE, PIECE)

    def along_x(i):
        k = far_first(i, NX)
        return k - 1, (x + k) % NX, device(y, (x + k) % NX, z, core)

    def scatter_x(i):
        ky = far_first(i, NY)
        y2 = (y + ky) % NY

        @pl.when(y2 < OWNERS)
        def _():
            def step(j):
                kx, x2, to = along_x(j)
                send(qp_v.at[piece(x2, y2)], rx_rx.at[kx, local_piece(y2)], rx_s, rx_r.at[kx, ky], to)

            loop(NX - 1, step)

    loop(NY, scatter_x)
    mean = mean_v[...]
    c_v[...] = dot(mean, mean, ((0,), (0,)), lax.Precision.HIGHEST)

    def scatter_y(i):
        ky = far_first(i, NY)
        y2 = (y + ky) % NY

        @pl.when(y2 < OWNERS)
        def _():
            value = qp_v[piece(x, y2), :]
            for kx in range(NX - 1):
                wait(rx_rx.at[kx, local_piece(y2)], rx_r.at[kx, ky])
                value = value + rx_rx[kx, local_piece(y2), :]
            ry_v[local_piece(y2), :] = value

            @pl.when(ky > 0)
            def _():
                send(ry_v.at[local_piece(y2)], ry_rx.at[ky - 1], ry_s, ry_r.at[ky - 1], along_y(i)[1])

    steps = rank // 8

    def stage(i):
        first = jnp.where(i == 0, 0, FIRST + i - 1)
        last = jnp.where(i == NY, steps, FIRST + i)
        c_v[...] = lax.fori_loop(first, last, panel, c_v[...])

        @pl.when(i < NY)
        def _():
            scatter_y(i)

    loop(NY + 1, stage)
    inverse = inverse_factor(c_v[...])

    def to_x(ref):
        loop(NX - 1, lambda j: send(ref, ref, gx_s, gx_r, along_x(j)[2]))

    @pl.when(y < OWNERS)
    def _():
        def add(i, value):
            wait(ry_rx.at[i], ry_r.at[i])
            return value + ry_rx[i]

        total = lax.fori_loop(0, NY - 1, add, ry_v[local_piece(y), :])
        right_v[piece(x, y), :] = times_transposed(total, inverse) / replicas
        out = right_v.at[piece(x, y)]
        loop(NY - 1, lambda i: send(out, out, gy_s, gy_r.at[along_y(i)[0] - 1], along_y(i)[1]))
        to_x(out)

    p_hat_out[...] = times_transposed(mean_v[...], inverse)
    sent = qp_v.at[pl.ds(0, (NX - 1) * OWNERS * PIECE)]
    wait(sent, rx_s)

    wait(ry_v.at[pl.ds(0, (OWNERS - 1) * PIECE)], ry_s)

    @pl.when(y >= OWNERS)
    def _():
        wait(ry_v.at[pl.ds(0, PIECE)], ry_s)

    def pass_on(i):
        ky = far_first(NY - 2 - i, NY)
        y2 = (y + NY - ky) % NY

        @pl.when(y2 < OWNERS)
        def _():
            got = right_v.at[piece(x, y2)]
            wait(got, gy_r.at[ky - 1])
            to_x(got)

    loop(NY - 1, pass_on)

    @pl.when(y < OWNERS)
    def _():
        wait(qp_v.at[pl.ds(0, (NY - 1) * PIECE)], gy_s)

    wait(sent, gx_r)
    wait(sent, gx_s)
    right_out[...] = right_v[...]


def finish(
    g_hbm, e_hbm, q_v, p_hat_v, approx_hbm, q_hbm, error_hbm,
    m_v, q3_v, approx_v, error_v, load_sems, q_sem, sems,
):
    _, rows, width = m_v.shape

    def load(i):
        block = span(i * BLOCK, BLOCK, 16)
        return [
            pltpu.make_async_copy(src.at[block], m_v.at[k, block], load_sems.at[k, i])
            for k, src in enumerate((g_hbm, e_hbm))
        ]

    loop(rows // BLOCK, lambda i: [copy.start() for copy in load(i)])
    q_copy = pltpu.make_async_copy(q_v, q_hbm, q_sem)
    q_copy.start()

    def right_rows(i):
        block = span(i * TALL, TALL, 16)
        high, low = halves(q_v[block, :])
        q3_v[block, :] = jnp.concatenate([high, high, low], axis=1)

    loop(width // TALL, right_rows)

    def stores(i):
        block = span(i * BLOCK, BLOCK, 16)
        return [
            pltpu.make_async_copy(src.at[block], dst.at[block], sems.at[k, i])
            for k, (src, dst) in enumerate(((approx_v, approx_hbm), (error_v, error_hbm)))
        ]

    def left_rows(i):
        block = span(i * BLOCK, BLOCK, 16)
        high, low = halves(p_hat_v[block, :])
        full = dot(jnp.concatenate([high, low, high], axis=1), q3_v[...], ((1,), (1,)))
        approx_v[block, :] = full.astype(BF16)
        for copy in load(i):
            copy.wait()
        error_v[block, :] = (m_v[0, block, :].astype(F32) + m_v[1, block, :].astype(F32) - full).astype(BF16)
        for copy in stores(i):
            copy.start()

    loop(rows // BLOCK, left_rows)
    loop(rows // BLOCK, lambda i: [copy.wait() for copy in stores(i)])
    q_copy.wait()


def local(grads, errors, q_start):
    grads, errors = grads[0], errors[0]
    rows, width = grads.shape
    rank = q_start.shape[1]
    chunk = rows // (NX * NC)
    cols = width // NX
    nxc = NX * NC - 1
    anywhere = pl.BlockSpec(memory_space=pl.ANY)
    vmem = pl.BlockSpec(memory_space=pltpu.VMEM)
    dma = pltpu.SemaphoreType.DMA
    right, p_hat = pl.pallas_call(
        exchange,
        out_shape=(
            jax.ShapeDtypeStruct((width, rank), F32),
            jax.ShapeDtypeStruct((rows, rank), F32),
        ),
        in_specs=[anywhere] * 3,
        out_specs=(vmem,) * 2,
        scratch_shapes=[
            pltpu.VMEM((2, rows, width), BF16),
            pltpu.VMEM((width, rank), F32),
            pltpu.VMEM((2, width, rows), BF16),
            pltpu.VMEM((rows, rank), F32),
            pltpu.VMEM((nxc, chunk, rank), F32),
            pltpu.VMEM((NY, SPLIT, rank), F32),
            pltpu.VMEM((NZ, chunk - SPLIT, rank), F32),
            pltpu.VMEM((NZ, SPLIT, rank), F32),
            pltpu.VMEM((NY, chunk - SPLIT, rank), F32),
            pltpu.VMEM((rows, rank), F32),
            pltpu.VMEM((rows, 2 * rank), BF16),
            pltpu.VMEM((width, rank), F32),
            pltpu.VMEM((NX - 1, cols, rank), F32),
            pltpu.VMEM((cols, rank), F32),
            pltpu.VMEM((NY - 1, PIECE, rank), F32),
            pltpu.VMEM((width, rank), F32),
            pltpu.VMEM((rank, rank), F32),
            dma((3,)),
            dma, dma((nxc,)),
            dma, dma, dma, dma, dma, dma, dma, dma,
            dma, dma,
            dma, dma((NX - 1, NY)),
            dma, dma((NY - 1,)),
            dma, dma((NY - 1,)),
            dma, dma,
        ],
        compiler_params=pltpu.CompilerParams(collective_id=0, has_side_effects=True, vmem_limit_bytes=LIMIT),
        name="exchange",
    )(grads, errors, q_start)

    approx, q_next, error_next = pl.pallas_call(
        finish,
        out_shape=(
            jax.ShapeDtypeStruct((rows, width), BF16),
            jax.ShapeDtypeStruct((width, rank), F32),
            jax.ShapeDtypeStruct((rows, width), BF16),
        ),
        in_specs=[anywhere] * 2 + [vmem] * 2,
        out_specs=(anywhere,) * 3,
        scratch_shapes=[
            pltpu.VMEM((2, rows, width), BF16),
            pltpu.VMEM((width, 3 * rank), BF16),
            pltpu.VMEM((rows, width), BF16),
            pltpu.VMEM((rows, width), BF16),
            dma((2, rows // BLOCK)),
            dma,
            dma((2, rows // BLOCK)),
        ],
        compiler_params=pltpu.CompilerParams(vmem_limit_bytes=LIMIT),
        name="finish",
    )(grads, errors, right, p_hat)
    return approx, q_next, error_next[None]


def solution(mesh):
    return jax.shard_map(
        local,
        mesh=mesh,
        in_specs=(P("dp", None, "mp"), P("dp", None, "mp"), P("mp", None)),
        out_specs=(P(None, "mp"), P("mp", None), P("dp", None, "mp")),
        check_vma=False,
    )
```

time: 65.9 us -> 61.1 us (0.927)
  Pallas kernels: 65.1 us -> 60.2 us
    pallas_call x1, Pallas kernels: 61 us -> 56.5 us  [local(): pl.pallas_call(exchange, out_shape=(jax.ShapeDtypeStruct((width, rank), F...]
where the time goes in v3:
time: 61.1 us; the launch traced here: 60.9 us
  Pallas kernels  60.2 us (99%)
  between operations  0.64 us (1%)
    pallas_call x1, Pallas kernels, local(): pl.pallas_call(exchange, out_shape=(jax.ShapeDtypeStruct((width, rank), F...  56.5 us
    pallas_call x1, Pallas kernels, local(): pl.pallas_call(finish, out_shape=(jax.ShapeDtypeStruct((rows, width), BF1...  3.7 us

profile of v3, /device:TPU:2, one launch (start us, length us, event | category | flops | bytes accessed | tf_op | source)
XLA Modules:
  0.0 60.9 jit_solution(14210988361686852134)
XLA Ops:
  0.6 56.5 %exchange.1 = (f32[1120,128]{1,0:T(8,128)S(1)}, f32[448,128]{1,0:T(8,128)S(1)}) custom-call(bf16[448,1120]{1,0:T(8,128)(2,1)} %bitcast.3, bf16[448,1120]{1,0:T(8,128)(2,1)} %bitcast.5, f32[1120,128]{1,0:T(8,128)} %q_hbm.1), custom_call_target="tpu_custom_call" | custom-call | tf_op jit(solution)/shard_map/exchange/pallas_call | solution.py:409
  57.2 3.7 %finish.1 = (bf16[448,1120]{1,0:T(8,128)(2,1)}, f32[1120,128]{1,0:T(8,128)}, bf16[448,1120]{1,0:T(8,128)(2,1)}) custom-call(bf16[448,1120]{1,0:T(8,128)(2,1)} %bitcast.4, bf16[448,1120]{1,0:T(8,128)(2,1)} %bitcast.6, f32[1120,128]{1,0:T(8,128)S(1)} %get-tuple-element.8.q_v, f32[448,128]{1,0:T(8,128)S(1)} %get-tuple-element.9.p_hat_v), custom_call_target="tpu_custom_call" | custom-call | tf_op jit(solution)/shard_map/finish/pallas_call | solution.py:448

commit v4 on v3

--- a/solution.py
+++ b/solution.py
@@ -18,7 +18,7 @@
 BLOCK = 112
 TALL = 224
 FIRST = 3
-LIMIT = 53 * 2**20
+LIMIT = 51 * 2**20
 
 
 def loop(n, body):
@@ -103,10 +103,10 @@
 
 
 def exchange(
-    g_hbm, e_hbm, q_hbm, right_out, p_hat_out,
-    m_v, q_v, t_v, part_v, a_rx, by_rx, bz_rx, dz_rx, dy_rx, mean_v, p2_v,
+    g_hbm, e_hbm, q_hbm, m_v, right_out, p_hat_out,
+    q_v, t_v, part_v, a_rx, by_rx, bz_rx, dz_rx, dy_rx, mean_v, p2_v,
     qp_v, rx_rx, ry_v, ry_rx, right_v, c_v,
-    load_sem, a_s, a_r, by_s, by_r, bz_s, bz_r, dz_s, dz_r, dy_s, dy_r, c_s, c_r,
+    q_sem, load_sem, a_s, a_r, by_s, by_r, bz_s, bz_r, dz_s, dz_r, dy_s, dy_r, c_s, c_r,
     rx_s, rx_r, ry_s, ry_r, gy_s, gy_r, gx_s, gx_r,
 ):
     _, rows, width = m_v.shape
@@ -143,12 +143,16 @@
         c2 = (core + NC - 1 - i % NC) % NC
         return x2 * NC + c2, device(y, x2, z, c2)
 
-    loads = [
-        pltpu.make_async_copy(src, dst, load_sem.at[i])
-        for i, (src, dst) in enumerate(((q_hbm, q_v), (g_hbm, m_v.at[0]), (e_hbm, m_v.at[1])))
-    ]
-    for load in loads:
-        load.start()
+    def load(i):
+        block = span(i * BLOCK, BLOCK, 16)
+        return [
+            pltpu.make_async_copy(src.at[block], m_v.at[k, block], load_sem.at[k, i])
+            for k, src in enumerate((g_hbm, e_hbm))
+        ]
+
+    q_load = pltpu.make_async_copy(q_hbm, q_v, q_sem)
+    q_load.start()
+    loop(rows // BLOCK, lambda i: [copy.start() for copy in load(i)])
 
     barrier = pltpu.get_barrier_semaphore()
 
@@ -158,12 +162,13 @@
     loop(max(NY, NZ) - 1, lambda i: (greet(along_y(i)[1]), greet(along_z(i)[1])))
     loop(nxc - 1, lambda i: greet(across(i)[1]))
 
-    for load in loads:
-        load.wait()
+    q_load.wait()
     q2 = jnp.concatenate(halves(q_v[...]), axis=1)
 
     def left_rows(i):
         block = span(i * BLOCK, BLOCK, 16)
+        for copy in load(i):
+            copy.wait()
         both = dot(m_v[0, block, :], q2) + dot(m_v[1, block, :], q2)
         part_v[block, :] = both[:, :rank] + both[:, rank:]
 
@@ -350,19 +355,11 @@
 
 
 def finish(
-    g_hbm, e_hbm, q_v, p_hat_v, approx_hbm, q_hbm, error_hbm,
-    m_v, q3_v, approx_v, error_v, load_sems, q_sem, sems,
+    m_v, q_v, p_hat_v, approx_hbm, q_hbm, error_hbm,
+    q3_v, approx_v, error_v, q_sem, sems,
 ):
     _, rows, width = m_v.shape
 
-    def load(i):
-        block = span(i * BLOCK, BLOCK, 16)
-        return [
-            pltpu.make_async_copy(src.at[block], m_v.at[k, block], load_sems.at[k, i])
-            for k, src in enumerate((g_hbm, e_hbm))
-        ]
-
-    loop(rows // BLOCK, lambda i: [copy.start() for copy in load(i)])
     q_copy = pltpu.make_async_copy(q_v, q_hbm, q_sem)
     q_copy.start()
 
@@ -385,8 +382,6 @@
         high, low = halves(p_hat_v[block, :])
         full = dot(jnp.concatenate([high, low, high], axis=1), q3_v[...], ((1,), (1,)))
         approx_v[block, :] = full.astype(BF16)
-        for copy in load(i):
-            copy.wait()
         error_v[block, :] = (m_v[0, block, :].astype(F32) + m_v[1, block, :].astype(F32) - full).astype(BF16)
         for copy in stores(i):
             copy.start()
@@ -406,16 +401,16 @@
     anywhere = pl.BlockSpec(memory_space=pl.ANY)
     vmem = pl.BlockSpec(memory_space=pltpu.VMEM)
     dma = pltpu.SemaphoreType.DMA
-    right, p_hat = pl.pallas_call(
+    merged, right, p_hat = pl.pallas_call(
         exchange,
         out_shape=(
-            jax.ShapeDtypeStruct((width, rank), F32),
-            jax.ShapeDtypeStruct((rows, rank), F32),
+            pltpu.VMEM((2, rows, width), BF16),
+            pltpu.VMEM((width, rank), F32),
+            pltpu.VMEM((rows, rank), F32),
         ),
         in_specs=[anywhere] * 3,
-        out_specs=(vmem,) * 2,
+        out_specs=(vmem,) * 3,
         scratch_shapes=[
-            pltpu.VMEM((2, rows, width), BF16),
             pltpu.VMEM((width, rank), F32),
             pltpu.VMEM((2, width, rows), BF16),
             pltpu.VMEM((rows, rank), F32),
@@ -432,7 +427,7 @@
             pltpu.VMEM((NY - 1, PIECE, rank), F32),
             pltpu.VMEM((width, rank), F32),
             pltpu.VMEM((rank, rank), F32),
-            dma((3,)),
+            dma, dma((2, rows // BLOCK)),
             dma, dma((nxc,)),
             dma, dma, dma, dma, dma, dma, dma, dma,
             dma, dma,
@@ -452,20 +447,18 @@
             jax.ShapeDtypeStruct((width, rank), F32),
             jax.ShapeDtypeStruct((rows, width), BF16),
         ),
-        in_specs=[anywhere] * 2 + [vmem] * 2,
+        in_specs=[vmem] * 3,
         out_specs=(anywhere,) * 3,
         scratch_shapes=[
-            pltpu.VMEM((2, rows, width), BF16),
             pltpu.VMEM((width, 3 * rank), BF16),
             pltpu.VMEM((rows, width), BF16),
             pltpu.VMEM((rows, width), BF16),
-            dma((2, rows // BLOCK)),
             dma,
             dma((2, rows // BLOCK)),
         ],
-        compiler_params=pltpu.CompilerParams(vmem_limit_bytes=LIMIT),
+        compiler_params=pltpu.CompilerParams(vmem_limit_bytes=LIMIT - 2**20),
         name="finish",
-    )(grads, errors, right, p_hat)
+    )(merged, right, p_hat)
     return approx, q_next, error_next[None]
 
 

time: 61.1 us -> 59.7 us (0.977)
  Pallas kernels: 60.2 us -> 58.9 us
    pallas_call x1, Pallas kernels: 3.7 us -> 2.63 us  [local(): pl.pallas_call(finish, out_shape=(jax.ShapeDtypeStruct((rows, width), BF1...]
where the time goes in v4:
time: 59.7 us; the launch traced here: 59.6 us
  Pallas kernels  58.9 us (99%)
  between operations  0.64 us (1%)
    pallas_call x1, Pallas kernels, local(): pl.pallas_call(exchange, out_shape=(pltpu.VMEM((2, rows, width), BF16), p...  56.3 us
    pallas_call x1, Pallas kernels, local(): pl.pallas_call(finish, out_shape=(jax.ShapeDtypeStruct((rows, width), BF1...  2.63 us

profile of v4, /device:TPU:2, one launch (start us, length us, event | category | flops | bytes accessed | tf_op | source)
XLA Modules:
  0.0 59.6 jit_solution(913988592785681802)
XLA Ops:
  0.6 56.3 %exchange.1 = (bf16[2,448,1120]{2,1,0:T(8,128)(2,1)S(1)}, f32[1120,128]{1,0:T(8,128)S(1)}, f32[448,128]{1,0:T(8,128)S(1)}) custom-call(bf16[448,1120]{1,0:T(8,128)(2,1)} %bitcast.3, bf16[448,1120]{1,0:T(8,128)(2,1)} %bitcast.4, f32[1120,128]{1,0:T(8,128)} %q_hbm.1), custom_call_target="tpu_custom_call" | custom-call | tf_op jit(solution)/shard_map/exchange/pallas_call | solution.py:404
  56.9 2.6 %finish.1 = (bf16[448,1120]{1,0:T(8,128)(2,1)}, f32[1120,128]{1,0:T(8,128)}, bf16[448,1120]{1,0:T(8,128)(2,1)}) custom-call(bf16[2,448,1120]{2,1,0:T(8,128)(2,1)S(1)} %get-tuple-element.9.m_v, f32[1120,128]{1,0:T(8,128)S(1)} %get-tuple-element.10.q_v, f32[448,128]{1,0:T(8,128)S(1)} %get-tuple-element.11.p_hat_v), custom_call_target="tpu_custom_call" | custom-call | tf_op jit(solution)/shard_map/finish/pallas_call | solution.py:443

commit v5 on v4

--- a/solution.py
+++ b/solution.py
@@ -12,12 +12,11 @@
 BF16 = jnp.bfloat16
 
 NX, NY, NZ, NC = 4, 8, 8, 2
-OWNERS = 7
-PIECE = 40
+PIECE, LONG, MORE = 32, 40, 3
 SPLIT = 32
 BLOCK = 112
 TALL = 224
-FIRST = 3
+FIRST = 5
 LIMIT = 51 * 2**20
 
 
@@ -30,7 +29,7 @@
 
 
 def far_first(i, n):
-    return n // 2 + (i + 1) // 2 * (1 - 2 * (i % 2))
+    return n // 2 + lax.div(i + 1, 2) * (1 - 2 * lax.rem(i, 2))
 
 
 def dot(a, b, dims=((1,), (0,)), precision=None):
@@ -117,7 +116,7 @@
     nxc = NX * NC
     dp = lax.axis_index("dp")
     mp = lax.axis_index("mp")
-    y, x, z, core = dp // NX, dp % NX, mp // NC, mp % NC
+    y, x, z, core = lax.div(dp, NX), lax.rem(dp, NX), lax.div(mp, NC), lax.rem(mp, NC)
 
     def device(y, x, z, core):
         return (y * NX + x, z * NC + core)
@@ -132,15 +131,15 @@
 
     def along_y(i):
         k = far_first(i, NY)
-        return k, device((y + k) % NY, x, z, core)
+        return k, device(lax.rem(y + k, NY), x, z, core)
 
     def along_z(i):
         k = far_first(i, NZ)
-        return k, device(y, x, (z + k) % NZ, core)
+        return k, device(y, x, lax.rem(z + k, NZ), core)
 
     def across(i):
-        x2 = (x + far_first(i // NC, NX)) % NX
-        c2 = (core + NC - 1 - i % NC) % NC
+        x2 = lax.rem(x + far_first(lax.div(i, NC), NX), NX)
+        c2 = lax.rem(core + NC - 1 - lax.rem(i, NC), NC)
         return x2 * NC + c2, device(y, x2, z, c2)
 
     def load(i):
@@ -187,8 +186,8 @@
     full = width // 128
 
     def turn(i):
-        at = span(i % full * 128, 128, 128)
-        t_v[i // full, at, :] = m_v[i // full, :, at].T
+        at = span(lax.rem(i, full) * 128, 128, 128)
+        t_v[lax.div(i, full), at, :] = m_v[lax.div(i, full), :, at].T
 
     loop(2 * full, turn)
     if width % 128:
@@ -252,27 +251,28 @@
 
     loop(width // TALL, right_rows)
 
-    def piece(x, y):
-        return span(x * cols + y * PIECE, PIECE)
-
-    def local_piece(y):
-        return span(y * PIECE, PIECE)
+    def for_piece(y, body):
+        pl.when(y < MORE)(lambda: body(y * LONG, LONG))
+        pl.when(y >= MORE)(lambda: body(y * PIECE + MORE * (LONG - PIECE), PIECE))
+
+    def whole(x, start, size):
+        return span(x * cols + start, size)
 
     def along_x(i):
         k = far_first(i, NX)
-        return k - 1, (x + k) % NX, device(y, (x + k) % NX, z, core)
+        return k - 1, lax.rem(x + k, NX), device(y, lax.rem(x + k, NX), z, core)
 
     def scatter_x(i):
         ky = far_first(i, NY)
-        y2 = (y + ky) % NY
-
-        @pl.when(y2 < OWNERS)
-        def _():
+
+        def body(start, size):
             def step(j):
                 kx, x2, to = along_x(j)
-                send(qp_v.at[piece(x2, y2)], rx_rx.at[kx, local_piece(y2)], rx_s, rx_r.at[kx, ky], to)
+                send(qp_v.at[whole(x2, start, size)], rx_rx.at[kx, span(start, size)], rx_s, rx_r.at[kx, ky], to)
 
             loop(NX - 1, step)
+
+        for_piece(lax.rem(y + ky, NY), body)
 
     loop(NY, scatter_x)
     mean = mean_v[...]
@@ -280,19 +280,21 @@
 
     def scatter_y(i):
         ky = far_first(i, NY)
-        y2 = (y + ky) % NY
-
-        @pl.when(y2 < OWNERS)
-        def _():
-            value = qp_v[piece(x, y2), :]
+
+        def body(start, size):
+            part = span(start, size)
+            value = qp_v[whole(x, start, size), :]
             for kx in range(NX - 1):
-                wait(rx_rx.at[kx, local_piece(y2)], rx_r.at[kx, ky])
-                value = value + rx_rx[kx, local_piece(y2), :]
-            ry_v[local_piece(y2), :] = value
+                wait(rx_rx.at[kx, part], rx_r.at[kx, ky])
+                value = value + rx_rx[kx, part, :]
+            ry_v[part, :] = value
 
             @pl.when(ky > 0)
             def _():
-                send(ry_v.at[local_piece(y2)], ry_rx.at[ky - 1], ry_s, ry_r.at[ky - 1], along_y(i)[1])
+                dst = ry_rx.at[ky - 1, pl.ds(0, size)]
+                send(ry_v.at[part], dst, ry_s, ry_r.at[ky - 1], along_y(i)[1])
+
+        for_piece(lax.rem(y + ky, NY), body)
 
     steps = rank // 8
 
@@ -311,44 +313,39 @@
     def to_x(ref):
         loop(NX - 1, lambda j: send(ref, ref, gx_s, gx_r, along_x(j)[2]))
 
-    @pl.when(y < OWNERS)
-    def _():
+    def gather_own(start, size):
         def add(i, value):
-            wait(ry_rx.at[i], ry_r.at[i])
-            return value + ry_rx[i]
-
-        total = lax.fori_loop(0, NY - 1, add, ry_v[local_piece(y), :])
-        right_v[piece(x, y), :] = times_transposed(total, inverse) / replicas
-        out = right_v.at[piece(x, y)]
+            wait(ry_rx.at[i, pl.ds(0, size)], ry_r.at[i])
+            return value + ry_rx[i, :size]
+
+        total = lax.fori_loop(0, NY - 1, add, ry_v[span(start, size), :])
+        right_v[whole(x, start, size), :] = times_transposed(total, inverse) / replicas
+        out = right_v.at[whole(x, start, size)]
+        to_x(out)
         loop(NY - 1, lambda i: send(out, out, gy_s, gy_r.at[along_y(i)[0] - 1], along_y(i)[1]))
-        to_x(out)
-
+
+    for_piece(y, gather_own)
     p_hat_out[...] = times_transposed(mean_v[...], inverse)
-    sent = qp_v.at[pl.ds(0, (NX - 1) * OWNERS * PIECE)]
+    sent = qp_v.at[pl.ds(0, (NX - 1) * cols)]
     wait(sent, rx_s)
-
-    wait(ry_v.at[pl.ds(0, (OWNERS - 1) * PIECE)], ry_s)
-
-    @pl.when(y >= OWNERS)
-    def _():
-        wait(ry_v.at[pl.ds(0, PIECE)], ry_s)
 
     def pass_on(i):
         ky = far_first(NY - 2 - i, NY)
-        y2 = (y + NY - ky) % NY
-
-        @pl.when(y2 < OWNERS)
-        def _():
-            got = right_v.at[piece(x, y2)]
+
+        def body(start, size):
+            got = right_v.at[whole(x, start, size)]
             wait(got, gy_r.at[ky - 1])
             to_x(got)
 
+        for_piece(lax.rem(y + NY - ky, NY), body)
+
     loop(NY - 1, pass_on)
 
-    @pl.when(y < OWNERS)
-    def _():
-        wait(qp_v.at[pl.ds(0, (NY - 1) * PIECE)], gy_s)
-
+    def sent_along_y(start, size):
+        wait(ry_v.at[pl.ds(0, cols - size)], ry_s)
+        wait(qp_v.at[pl.ds(0, (NY - 1) * size)], gy_s)
+
+    for_piece(y, sent_along_y)
     wait(sent, gx_r)
     wait(sent, gx_s)
     right_out[...] = right_v[...]
@@ -424,7 +421,7 @@
             pltpu.VMEM((width, rank), F32),
             pltpu.VMEM((NX - 1, cols, rank), F32),
             pltpu.VMEM((cols, rank), F32),
-            pltpu.VMEM((NY - 1, PIECE, rank), F32),
+            pltpu.VMEM((NY - 1, LONG, rank), F32),
             pltpu.VMEM((width, rank), F32),
             pltpu.VMEM((rank, rank), F32),
             dma, dma((2, rows // BLOCK)),

time: 59.7 us -> 59.8 us (level)
  no operation moved by 1% of the time
where the time goes in v5:
time: 59.8 us; the launch traced here: 59.7 us
  Pallas kernels  59 us (99%)
  between operations  0.64 us (1%)
    pallas_call x1, Pallas kernels, local(): pl.pallas_call(exchange, out_shape=(pltpu.VMEM((2, rows, width), BF16), p...  56.4 us
    pallas_call x1, Pallas kernels, local(): pl.pallas_call(finish, out_shape=(jax.ShapeDtypeStruct((rows, width), BF1...  2.61 us

profile of v5, /device:TPU:2, one launch (start us, length us, event | category | flops | bytes accessed | tf_op | source)
XLA Modules:
  0.0 59.7 jit_solution(9030406984720595924)
XLA Ops:
  0.6 56.4 %exchange.1 = (bf16[2,448,1120]{2,1,0:T(8,128)(2,1)S(1)}, f32[1120,128]{1,0:T(8,128)S(1)}, f32[448,128]{1,0:T(8,128)S(1)}) custom-call(bf16[448,1120]{1,0:T(8,128)(2,1)} %bitcast.3, bf16[448,1120]{1,0:T(8,128)(2,1)} %bitcast.4, f32[1120,128]{1,0:T(8,128)} %q_hbm.1), custom_call_target="tpu_custom_call" | custom-call | tf_op jit(solution)/shard_map/exchange/pallas_call | solution.py:401
  57.1 2.6 %finish.1 = (bf16[448,1120]{1,0:T(8,128)(2,1)}, f32[1120,128]{1,0:T(8,128)}, bf16[448,1120]{1,0:T(8,128)(2,1)}) custom-call(bf16[2,448,1120]{2,1,0:T(8,128)(2,1)S(1)} %get-tuple-element.9.m_v, f32[1120,128]{1,0:T(8,128)S(1)} %get-tuple-element.10.q_v, f32[448,128]{1,0:T(8,128)S(1)} %get-tuple-element.11.p_hat_v), custom_call_target="tpu_custom_call" | custom-call | tf_op jit(solution)/shard_map/finish/pallas_call | solution.py:440

commit v6 on v5

--- a/solution.py
+++ b/solution.py
@@ -17,6 +17,7 @@
 BLOCK = 112
 TALL = 224
 FIRST = 5
+WIDE = 256
 LIMIT = 51 * 2**20
 
 
@@ -246,7 +247,8 @@
 
     def right_rows(i):
         block = span(i * TALL, TALL, 16)
-        both = dot(t_v[0, block, :], p2_v[...]) + dot(t_v[1, block, :], p2_v[...])
+        both = dot(t_v[:, block, :].reshape(2 * TALL, rows), p2_v[...])
+        both = both[:TALL] + both[TALL:]
         qp_v[block, :] = both[:, :rank] + both[:, rank:]
 
     loop(width // TALL, right_rows)
@@ -353,38 +355,35 @@
 
 def finish(
     m_v, q_v, p_hat_v, approx_hbm, q_hbm, error_hbm,
-    q3_v, approx_v, error_v, q_sem, sems,
+    p3_v, approx_v, error_v, q_sem, sems,
 ):
     _, rows, width = m_v.shape
-
     q_copy = pltpu.make_async_copy(q_v, q_hbm, q_sem)
     q_copy.start()
-
-    def right_rows(i):
-        block = span(i * TALL, TALL, 16)
-        high, low = halves(q_v[block, :])
-        q3_v[block, :] = jnp.concatenate([high, high, low], axis=1)
-
-    loop(width // TALL, right_rows)
-
-    def stores(i):
-        block = span(i * BLOCK, BLOCK, 16)
+    high, low = halves(p_hat_v[...])
+    p3_v[...] = jnp.concatenate([high, low, high], axis=1)
+
+    def stores(i, columns):
         return [
-            pltpu.make_async_copy(src.at[block], dst.at[block], sems.at[k, i])
+            pltpu.make_async_copy(src.at[:, columns], dst.at[:, columns], sems.at[k, i])
             for k, (src, dst) in enumerate(((approx_v, approx_hbm), (error_v, error_hbm)))
         ]
 
-    def left_rows(i):
-        block = span(i * BLOCK, BLOCK, 16)
-        high, low = halves(p_hat_v[block, :])
-        full = dot(jnp.concatenate([high, low, high], axis=1), q3_v[...], ((1,), (1,)))
-        approx_v[block, :] = full.astype(BF16)
-        error_v[block, :] = (m_v[0, block, :].astype(F32) + m_v[1, block, :].astype(F32) - full).astype(BF16)
-        for copy in stores(i):
+    def tile(i, columns):
+        high, low = halves(q_v[columns, :])
+        full = dot(p3_v[...], jnp.concatenate([high, high, low], axis=1), ((1,), (1,)))
+        approx_v[:, columns] = full.astype(BF16)
+        error_v[:, columns] = (m_v[0, :, columns].astype(F32) + m_v[1, :, columns].astype(F32) - full).astype(BF16)
+        for copy in stores(i, columns):
             copy.start()
 
-    loop(rows // BLOCK, left_rows)
-    loop(rows // BLOCK, lambda i: [copy.wait() for copy in stores(i)])
+    tiles = width // WIDE
+    rest = pl.ds(tiles * WIDE, width - tiles * WIDE)
+    tile(tiles, rest)
+    loop(tiles, lambda i: tile(i, span(i * WIDE, WIDE, 128)))
+    loop(tiles, lambda i: [copy.wait() for copy in stores(i, span(i * WIDE, WIDE, 128))])
+    for copy in stores(tiles, rest):
+        copy.wait()
     q_copy.wait()
 
 
@@ -447,11 +446,11 @@
         in_specs=[vmem] * 3,
         out_specs=(anywhere,) * 3,
         scratch_shapes=[
-            pltpu.VMEM((width, 3 * rank), BF16),
+            pltpu.VMEM((rows, 3 * rank), BF16),
             pltpu.VMEM((rows, width), BF16),
             pltpu.VMEM((rows, width), BF16),
             dma,
-            dma((2, rows // BLOCK)),
+            dma((2, width // WIDE + 1)),
         ],
         compiler_params=pltpu.CompilerParams(vmem_limit_bytes=LIMIT - 2**20),
         name="finish",

time: 59.8 us -> 59.5 us (level)
  no operation moved by 1% of the time
where the time goes in v6:
time: 59.5 us; the launch traced here: 59.4 us
  Pallas kernels  58.8 us (99%)
  between operations  0.64 us (1%)
    pallas_call x1, Pallas kernels, local(): pl.pallas_call(exchange, out_shape=(pltpu.VMEM((2, rows, width), BF16), p...  56.4 us
    pallas_call x1, Pallas kernels, local(): pl.pallas_call(finish, out_shape=(jax.ShapeDtypeStruct((rows, width), BF1...  2.35 us

profile of v6, /device:TPU:2, one launch (start us, length us, event | category | flops | bytes accessed | tf_op | source)
XLA Modules:
  0.0 59.4 jit_solution(11355374511297916387)
XLA Ops:
  0.6 56.4 %exchange.1 = (bf16[2,448,1120]{2,1,0:T(8,128)(2,1)S(1)}, f32[1120,128]{1,0:T(8,128)S(1)}, f32[448,128]{1,0:T(8,128)S(1)}) custom-call(bf16[448,1120]{1,0:T(8,128)(2,1)} %bitcast.3, bf16[448,1120]{1,0:T(8,128)(2,1)} %bitcast.4, f32[1120,128]{1,0:T(8,128)} %q_hbm.1), custom_call_target="tpu_custom_call" | custom-call | tf_op jit(solution)/shard_map/exchange/pallas_call | solution.py:400
  57.0 2.3 %finish.1 = (bf16[448,1120]{1,0:T(8,128)(2,1)}, f32[1120,128]{1,0:T(8,128)}, bf16[448,1120]{1,0:T(8,128)(2,1)}) custom-call(bf16[2,448,1120]{2,1,0:T(8,128)(2,1)S(1)} %get-tuple-element.9.m_v, f32[1120,128]{1,0:T(8,128)S(1)} %get-tuple-element.10.q_v, f32[448,128]{1,0:T(8,128)S(1)} %get-tuple-element.11.p_hat_v), custom_call_target="tpu_custom_call" | custom-call | tf_op jit(solution)/shard_map/finish/pallas_call | solution.py:439

commit v7 on v6

--- a/solution.py
+++ b/solution.py
@@ -230,11 +230,13 @@
     loop(NZ - 1, functools.partial(spread_z, dz_rx, dz_s, dz_r))
     dy_rx[y] = collect(bz_rx, bz_r)
     loop(NY - 1, functools.partial(spread_y, dy_rx, dy_s, dy_r))
-    mean_v[span(mine * chunk, SPLIT), :] = collect(dz_rx, dz_r) / replicas
-    mean_v[span(mine * chunk + SPLIT, chunk - SPLIT), :] = collect(dy_rx, dy_r) / replicas
-
-    own = mean_v.at[span(mine * chunk, chunk)]
-    loop(nxc - 1, lambda i: send(own, own, c_s, c_r, across(i)[1]))
+    def gather(start, size, value):
+        mean_v[span(start, size), :] = value / replicas
+        own = mean_v.at[span(start, size)]
+        loop(nxc - 1, lambda i: send(own, own, c_s, c_r, across(i)[1]))
+
+    gather(mine * chunk, SPLIT, collect(dz_rx, dz_r))
+    gather(mine * chunk + SPLIT, chunk - SPLIT, collect(dy_rx, dy_r))
 
     wait(part_v.at[pl.ds(0, (nxc - 1) * chunk)], a_s)
     wait(by_rx.at[: NY - 1], by_s)

time: 59.5 us -> 59.4 us (level)
  no operation moved by 1% of the time
where the time goes in v7:
time: 59.4 us; the launch traced here: 59.2 us
  Pallas kernels  58.6 us (99%)
  between operations  0.64 us (1%)
    pallas_call x1, Pallas kernels, local(): pl.pallas_call(exchange, out_shape=(pltpu.VMEM((2, rows, width), BF16), p...  56.2 us
    pallas_call x1, Pallas kernels, local(): pl.pallas_call(finish, out_shape=(jax.ShapeDtypeStruct((rows, width), BF1...  2.35 us

profile of v7, /device:TPU:2, one launch (start us, length us, event | category | flops | bytes accessed | tf_op | source)
XLA Modules:
  0.0 59.2 jit_solution(3198926217523043065)
XLA Ops:
  0.6 56.2 %exchange.1 = (bf16[2,448,1120]{2,1,0:T(8,128)(2,1)S(1)}, f32[1120,128]{1,0:T(8,128)S(1)}, f32[448,128]{1,0:T(8,128)S(1)}) custom-call(bf16[448,1120]{1,0:T(8,128)(2,1)} %bitcast.3, bf16[448,1120]{1,0:T(8,128)(2,1)} %bitcast.4, f32[1120,128]{1,0:T(8,128)} %q_hbm.1), custom_call_target="tpu_custom_call" | custom-call | tf_op jit(solution)/shard_map/exchange/pallas_call | solution.py:402
  56.9 2.3 %finish.1 = (bf16[448,1120]{1,0:T(8,128)(2,1)}, f32[1120,128]{1,0:T(8,128)}, bf16[448,1120]{1,0:T(8,128)(2,1)}) custom-call(bf16[2,448,1120]{2,1,0:T(8,128)(2,1)S(1)} %get-tuple-element.9.m_v, f32[1120,128]{1,0:T(8,128)S(1)} %get-tuple-element.10.q_v, f32[448,128]{1,0:T(8,128)S(1)} %get-tuple-element.11.p_hat_v), custom_call_target="tpu_custom_call" | custom-call | tf_op jit(solution)/shard_map/finish/pallas_call | solution.py:441
